TPU v7x, 32 devices: a whole 2x2x4 slice. The times are simulated.
32 devices in a mesh: ctx: 8 (over z, y), head: 4 (over x, core).
Axes of the slice: x: 2, y: 2, z: 4, core: 2. Of those that a mesh axis runs over, the one named last changes fastest.
Arguments:
- queries: bfloat16 [2048, 2048], P('ctx', 'head'), may hold values from -6 to 6
- keys: bfloat16 [2048, 2048], P('ctx', 'head'), may hold values from -6 to 6
- values: bfloat16 [2048, 2048], P('ctx', 'head'), may hold values from -6 to 6
- out_grad: bfloat16 [2048, 2048], P('ctx', 'head'), may hold values from -6 to 6
- doc_lengths: int32 [8], replicated, may hold values from 1 to 768, as said below
Outputs:
- attended: float32 [2048, 2048], P('ctx', 'head')
- query_grad: float32 [2048, 2048], P('ctx', 'head')
- key_grad: float32 [2048, 2048], P('ctx', 'head')
- value_grad: float32 [2048, 2048], P('ctx', 'head')
Inputs may be any that keep to these rules, and one draw needn't show every extreme that they name: `doc_lengths`: the first document has exactly 768 tokens, every other one 1 to 768, and all lengths sum to 2048.
All inputs are finite; a program needn't handle non-finite values.
Results may differ from a plain program's by a relative error of at most 0.0095.
Values may be sent and summed in bfloat16 or wider, within the bound.
A program may use at most 64 MiB of HBM per device.

v0:
```python
import functools
import math

import jax
import jax.numpy as jnp
from jax import lax
from jax.experimental import pallas as pl
from jax.experimental.pallas import tpu as pltpu
from jax.sharding import PartitionSpec as P

HD = 128
PROMPT = 64
DOC_MOST = 768
REACH = 3
NEG_FILL = -1e30
SCALE = 1.0 / math.sqrt(HD)
SCALE2 = SCALE * math.log2(math.e)
MESH = pl.DeviceIdType.MESH


def remote(src, dst, send_sem, recv_sem, target):
    return pltpu.make_async_remote_copy(
        src_ref=src,
        dst_ref=dst,
        send_sem=send_sem,
        recv_sem=recv_sem,
        device_id={"ctx": target},
        device_id_type=MESH,
    )


def dot_nt(a, b):
    return lax.dot_general(a, b, (((1,), (1,)), ((), ())), preferred_element_type=jnp.float32)


def dot_nn(a, b):
    return jnp.dot(a, b, preferred_element_type=jnp.float32)


def dot_tn(a, b):
    return lax.dot_general(a, b, (((0,), (0,)), ((), ())), preferred_element_type=jnp.float32)


def kernel(
    n, first, far, len_ref, q_hbm, k_hbm, v_hbm, g_hbm,
    att_ref, dq_ref, dk_ref, dv_ref,
    q_ref, k_ref, v_ref, g_ref, kv_buf, qd_buf, rl_buf, pr_buf, pg_out, pg_buf, ld_own, ld_buf,
    s_buf, sp_buf, top_ref, tot_ref, out_t, dq_t,
    kv_ss, kv_rs, qd_ss, qd_rs, ld_ss, ld_rs, pr_ss, pr_rs, pg_ss, pg_rs, rl_ss, rl_rs, in_sem,
):
    rows, width = q_ref.shape
    heads = width // HD
    docs = len_ref.shape[0]
    me = lax.axis_index("ctx")
    later = n - first
    reach = max(far, first - 1)
    chunks = [pl.ds(c * PROMPT, PROMPT) for c in range(rows // PROMPT)]

    def has_before(d):
        near = (me >= d) & (me < first)
        return near | (me >= first + d) if d <= far else near

    def has_after(d):
        near = me + d < first
        return near | ((me >= first) & (me + d < n)) if d <= far else near

    own_copies = [
        pltpu.make_async_copy(src, dst, in_sem.at[i])
        for i, (src, dst) in enumerate(
            ((q_hbm, q_ref), (k_hbm, k_ref), (v_hbm, v_ref), (g_hbm, g_ref))
        )
    ]
    for copy in own_copies:
        copy.start()

    barrier = pltpu.get_barrier_semaphore()
    for s in range(1, n):
        pl.semaphore_signal(
            barrier, inc=1, device_id={"ctx": lax.rem(me + s, n)}, device_id_type=MESH
        )
    pl.semaphore_wait(barrier, n - 1)

    def kv_copy(d, w, c):
        src = (k_hbm, v_hbm)[w]
        return remote(
            src.at[chunks[c]], kv_buf.at[d - 1, w, chunks[c]],
            kv_ss.at[d - 1, w, c], kv_rs.at[d - 1, w, c], lax.rem(me + d, n),
        )

    def qd_copy(d, w, c):
        src = (q_hbm, g_hbm)[w]
        return remote(
            src.at[chunks[c]], qd_buf.at[d - 1, w, chunks[c]],
            qd_ss.at[d - 1, w, c], qd_rs.at[d - 1, w, c], lax.rem(me + n - d, n),
        )

    def qd_to_relay(w, c):
        src = (q_hbm, g_hbm)[w]
        return remote(
            src.at[chunks[c]], rl_buf.at[w, chunks[c]], qd_ss.at[0, w, c], rl_rs.at[w, c], first
        )

    def qd_relayed(w, c):
        return remote(
            rl_buf.at[w, chunks[c]], qd_buf.at[0, w, chunks[c]],
            rl_ss.at[w, c], qd_rs.at[0, w, c], first - 2,
        )

    parts = [(w, c) for c in range(len(chunks)) for w in (0, 1)]

    def ld_copy(d):
        return remote(
            ld_own, ld_buf.at[d - 1], ld_ss.at[d - 1], ld_rs.at[d - 1], lax.rem(me + n - d, n)
        )

    def pr_copy(src, w):
        return remote(src, pr_buf.at[w], pr_ss.at[w], pr_rs.at[w], lax.rem(me + 2, n))

    def pg_copy():
        slot = lax.rem(me + n - first, n)
        return remote(pg_out, pg_buf.at[slot], pg_ss, pg_rs.at[slot], 0)

    distances = range(1, reach + 1)

    for c in range(len(chunks)):
        for d in distances:
            @pl.when(has_after(d))
            def _(d=d, c=c):
                for w in (0, 1):
                    kv_copy(d, w, c).start()

    @pl.when(me == first - 1)
    def _():
        for w, c in parts:
            qd_to_relay(w, c).start()
            for d in range(2, first):
                qd_copy(d, w, c).start()

    for holder in (first - 2, first - 1):
        @pl.when(me == holder)
        def _(holder=holder):
            for w in (0, 1):
                kv_copy(holder, w, 0).wait_recv()
                pr_copy(kv_buf.at[holder - 1, w, pl.ds(0, PROMPT)], w).start()

    def pass_prompt():
        for w in (0, 1):
            pr_copy(pr_buf.at[w], w).wait_recv()

            @pl.when(me + 2 < n)
            def _(w=w):
                pr_copy(pr_buf.at[w], w).start()

    @pl.when(me == first)
    def _():
        def relay(some):
            for w, c in some:
                remote(
                    rl_buf.at[w, chunks[c]], rl_buf.at[w, chunks[c]],
                    rl_ss.at[w, c], rl_rs.at[w, c], first - 1,
                ).wait_recv()
                qd_relayed(w, c).start()

        relay(parts[: len(parts) // 2])
        pass_prompt()
        relay(parts[len(parts) // 2 :])

    for copy in own_copies:
        copy.wait()

    def doc_start(pos):
        start = jnp.zeros_like(pos)
        end = jnp.int32(0)
        for i in range(docs):
            end = end + len_ref[i]
            start = jnp.where(pos >= end, end, start)
        return start

    u_pos = me * rows + lax.broadcasted_iota(jnp.int32, (rows, 1), 0)
    t_pos = me * rows + lax.broadcasted_iota(jnp.int32, (1, rows), 1)
    t_start = doc_start(t_pos)

    def hs(h):
        return pl.ds(pl.multiple_of(h * HD, HD), HD)

    def forward(h, keys, values, mask):
        s = dot_nt(keys, q_ref[:, hs(h)]) * SCALE2
        if mask is not None:
            s = jnp.where(mask, s, NEG_FILL)
        top = top_ref[pl.ds(h, 1)]
        fresh = jnp.maximum(top, jnp.max(s, axis=0, keepdims=True))
        fade = jnp.exp2(top - fresh)
        p = jnp.exp2(s - fresh)
        top_ref[pl.ds(h, 1)] = fresh
        tot_ref[pl.ds(h, 1)] = tot_ref[pl.ds(h, 1)] * fade + jnp.sum(p, axis=0, keepdims=True)
        out_t[h] = out_t[h] * fade + dot_tn(values, p.astype(jnp.bfloat16))
        return s

    own_mask = (u_pos <= t_pos) & (u_pos >= t_start)

    @pl.loop(0, heads, unroll=2)
    def _(h):
        s = dot_nt(k_ref[:, hs(h)], q_ref[:, hs(h)]) * SCALE2
        s = jnp.where(own_mask, s, NEG_FILL)
        top = jnp.max(s, axis=0, keepdims=True)
        p = jnp.exp2(s - top)
        s_buf[0, h] = s
        top_ref[pl.ds(h, 1)] = top
        tot_ref[pl.ds(h, 1)] = jnp.sum(p, axis=0, keepdims=True)
        out_t[h] = dot_tn(v_ref[:, hs(h)], p.astype(jnp.bfloat16))

    @pl.when(me > first)
    def _():
        pass_prompt()

    @pl.when(me >= first)
    def _():
        @pl.loop(0, heads, unroll=2)
        def _(h):
            sp_buf[h] = forward(h, pr_buf[0, :, hs(h)], pr_buf[1, :, hs(h)], None)

    for d in distances:
        @pl.when(has_before(d))
        def _(d=d):
            for w, c in parts:
                if c == 0 and d in (first - 2, first - 1):
                    @pl.when(me != d)
                    def _(w=w):
                        kv_copy(d, w, 0).wait_recv()
                else:
                    kv_copy(d, w, c).wait_recv()
            if d == 1:
                for e in distances:
                    @pl.when(has_before(e) & (me != first - 1))
                    def _(e=e):
                        for w, c in parts:
                            qd_copy(e, w, c).start()
            mask = u_pos - d * rows >= t_start

            @pl.loop(0, heads, unroll=2)
            def _(h):
                s_buf[d, h] = forward(
                    h, kv_buf[d - 1, 0, :, hs(h)], kv_buf[d - 1, 1, :, hs(h)], mask
                )

    @pl.loop(0, heads, unroll=2)
    def _(h):
        total = tot_ref[pl.ds(h, 1)]
        out = out_t[h] / total
        att_ref[:, hs(h)] = jnp.transpose(out)
        grad = jnp.transpose(g_ref[:, hs(h)].astype(jnp.float32))
        ld_own[pl.ds(h, 1)] = top_ref[pl.ds(h, 1)] + jnp.log2(total)
        ld_own[pl.ds(heads + h, 1)] = jnp.sum(out * grad, axis=0, keepdims=True)

    for d in distances:
        @pl.when(has_before(d))
        def _(d=d):
            ld_copy(d).start()

    def backward(s, g, lse, delta, values):
        p = jnp.exp2(s - lse)
        dp = dot_nt(values, g)
        return p.astype(jnp.bfloat16), (p * (dp - delta)).astype(jnp.bfloat16)

    def own_backward(h, s, values):
        return backward(
            s, g_ref[:, hs(h)], ld_own[pl.ds(h, 1)], ld_own[pl.ds(heads + h, 1)], values
        )

    @pl.when(me >= first)
    def _():
        @pl.loop(0, heads, unroll=2)
        def _(h):
            p, ds = own_backward(h, sp_buf[h], pr_buf[1, :, hs(h)])
            pg_out[0, :, hs(h)] = dot_nn(ds, q_ref[:, hs(h)]).astype(jnp.bfloat16)
            pg_out[1, :, hs(h)] = dot_nn(p, g_ref[:, hs(h)]).astype(jnp.bfloat16)
            dq_t[h] = dot_tn(pr_buf[0, :, hs(h)], ds)

        pg_copy().start()

    @pl.when(me < first)
    def _():
        dq_t[...] = jnp.zeros_like(dq_t)

    @pl.loop(0, heads, unroll=2)
    def _(h):
        p, ds = own_backward(h, s_buf[0, h], v_ref[:, hs(h)])
        dk_ref[:, hs(h)] = dot_nn(ds, q_ref[:, hs(h)])
        dv_ref[:, hs(h)] = dot_nn(p, g_ref[:, hs(h)])
        dq_t[h] += dot_tn(k_ref[:, hs(h)], ds)

    for d in distances:
        @pl.when(has_before(d))
        def _(d=d):
            @pl.loop(0, heads, unroll=2)
            def _(h):
                p, ds = own_backward(h, s_buf[d, h], kv_buf[d - 1, 1, :, hs(h)])
                dq_t[h] += dot_tn(kv_buf[d - 1, 0, :, hs(h)], ds)

    @pl.loop(0, heads, unroll=2)
    def _(h):
        dq_ref[:, hs(h)] = jnp.transpose(dq_t[h] * SCALE)

    for d in distances:
        @pl.when(has_after(d))
        def _(d=d):
            for w, c in parts:
                qd_copy(d, w, c).wait_recv()
            ld_copy(d).wait_recv()
            mask = u_pos >= doc_start(t_pos + d * rows)

            @pl.loop(0, heads, unroll=2)
            def _(h):
                q = qd_buf[d - 1, 0, :, hs(h)]
                g = qd_buf[d - 1, 1, :, hs(h)]
                s = jnp.where(mask, dot_nt(k_ref[:, hs(h)], q) * SCALE2, NEG_FILL)
                p, ds = backward(
                    s, g, ld_buf[d - 1, pl.ds(h, 1)], ld_buf[d - 1, pl.ds(heads + h, 1)],
                    v_ref[:, hs(h)],
                )
                dk_ref[:, hs(h)] += dot_nn(ds, q)
                dv_ref[:, hs(h)] += dot_nn(p, g)

    @pl.when(me == 0)
    def _():
        @pl.loop(0, later)
        def _(i):
            remote(pg_out, pg_buf.at[i], pg_ss, pg_rs.at[i], 0).wait_recv()
            dk_ref[pl.ds(0, PROMPT)] += pg_buf[i, 0].astype(jnp.float32)
            dv_ref[pl.ds(0, PROMPT)] += pg_buf[i, 1].astype(jnp.float32)

    dk_ref[...] = dk_ref[...] * SCALE

    for d in distances:
        @pl.when(has_after(d))
        def _(d=d):
            for w, c in parts:
                kv_copy(d, w, c).wait_send()

        @pl.when(has_before(d))
        def _(d=d):
            for w, c in parts:
                qd_copy(d, w, c).wait_send()
            ld_copy(d).wait_send()

    @pl.when(me == first)
    def _():
        for w, c in parts:
            qd_relayed(w, c).wait_send()

    @pl.when((me >= first - 2) & (me + 2 < n))
    def _():
        for w in (0, 1):
            pr_copy(pr_buf.at[w], w).wait_send()

    @pl.when(me >= first)
    def _():
        pg_copy().wait_send()


def attention(far, queries, keys, values, out_grad, doc_lengths):
    rows, width = queries.shape
    heads = width // HD
    n = lax.axis_size("ctx")
    first = DOC_MOST // rows
    later = n - first
    reach = max(far, first - 1)
    cuts = rows // PROMPT
    bf, f32 = jnp.bfloat16, jnp.float32
    vmem = pl.BlockSpec(memory_space=pltpu.VMEM)
    hbm = pl.BlockSpec(memory_space=pltpu.HBM)
    dma = pltpu.SemaphoreType.DMA
    tile = rows * rows * heads
    out = jax.ShapeDtypeStruct((rows, width), f32)
    return pl.pallas_call(
        functools.partial(kernel, n, first, far),
        out_shape=[out] * 4,
        in_specs=[pl.BlockSpec(memory_space=pltpu.SMEM)] + [hbm] * 4,
        out_specs=[vmem] * 4,
        scratch_shapes=[pltpu.VMEM((rows, width), bf)] * 4
        + [
            pltpu.VMEM((reach, 2, rows, width), bf),
            pltpu.VMEM((reach, 2, rows, width), bf),
            pltpu.VMEM((2, rows, width), bf),
            pltpu.VMEM((2, PROMPT, width), bf),
            pltpu.VMEM((2, PROMPT, width), bf),
            pltpu.VMEM((later, 2, PROMPT, width), bf),
            pltpu.VMEM((2 * heads, rows), f32),
            pltpu.VMEM((reach, 2 * heads, rows), f32),
            pltpu.VMEM((reach + 1, heads, rows, rows), f32),
            pltpu.VMEM((heads, PROMPT, rows), f32),
            pltpu.VMEM((heads, rows), f32),
            pltpu.VMEM((heads, rows), f32),
            pltpu.VMEM((heads, HD, rows), f32),
            pltpu.VMEM((heads, HD, rows), f32),
            dma((reach, 2, cuts)), dma((reach, 2, cuts)),
            dma((reach, 2, cuts)), dma((reach, 2, cuts)),
            dma((reach,)), dma((reach,)),
            dma((2,)), dma((2,)),
            dma(()), dma((later,)),
            dma((2, cuts)), dma((2, cuts)), dma((4,)),
        ],
        compiler_params=pltpu.CompilerParams(
            collective_id=far, has_side_effects=True, vmem_limit_bytes=48 * 2**20
        ),
        cost_estimate=pl.CostEstimate(
            flops=2 * 8 * 4 * tile * HD, bytes_accessed=12 * rows * width, transcendentals=8 * tile
        ),
    )(doc_lengths, queries, keys, values, out_grad)


def on_device(queries, keys, values, out_grad, doc_lengths):
    rows = queries.shape[0]
    docs = doc_lengths.shape[0]
    order = jnp.arange(docs)
    ends = jnp.sum(jnp.where(order[:, None] <= order[None, :], doc_lengths[:, None], 0), axis=0)
    span = (ends - 1) // rows - (ends - doc_lengths) // rows
    far = jnp.any((span > 1) & (order > 0))
    return lax.cond(
        far,
        functools.partial(attention, REACH),
        functools.partial(attention, 1),
        queries, keys, values, out_grad, doc_lengths,
    )


def solution(mesh):
    block = P("ctx", "head")
    return jax.shard_map(
        on_device, mesh=mesh, in_specs=(block,) * 4 + (P(),), out_specs=(block,) * 4, check_vma=False
    )
```

profile of v0, /device:TPU:0, one launch (start us, length us, event | category | flops | bytes accessed | tf_op | source)
XLA Modules:
  0.0 49.7 jit_solution(16004918361375061196)
XLA Ops:
  0.6 0.0 copy-start
  0.6 0.6 %copy-done = s32[8]{0:T(128)S(1)} copy-done((s32[8]{0:T(128)S(1)}, s32[8]{0:T(128)}, u32[]{:S(2)}) %copy-start) | copy-done | bytes 56
  1.3 0.1 select_reduce_fusion
  1.4 0.6 %and_reduce_fusion = pred[]{:T(512)} fusion(s32[8]{0:T(128)S(1)} %select_reduce_fusion, s32[8]{0:T(128)S(1)} %copy-done), kind=kLoop, calls=%fused_computation.2 | loop fusion | flops 295 | bytes 65 | tf_op jit(solution)/shard_map/reduce_or | solution.py:418
  2.7 43.8 %conditional.1 = ((f32[256,512]{1,0:T(8,128)S(1)}, f32[256,512]{1,0:T(8,128)S(1)}, f32[256,512]{1,0:T(8,128)S(1)}, f32[256,512]{1,0:T(8,128)S(1)})) conditional(s32[]{:T(128)} %convert_element_type.3, (s32[8]{0:T(128)S(1)}, bf16[256,512]{1,0:T(8,128)(2,1)}, bf16[256,512]{1,0:T(8,128)(2,1)}, bf16[256,512]{1,0:T(8,128)(2,1)}, ...), branch_computations={%region_2.3_spmd, %region_3.4_spmd} | conditional | flops 2147483648 | bytes 1572872 | solution.py:419
  2.7 43.8 %branch_0_fun.1 = (f32[256,512]{1,0:T(8,128)S(1)}, f32[256,512]{1,0:T(8,128)S(1)}, f32[256,512]{1,0:T(8,128)S(1)}, f32[256,512]{1,0:T(8,128)S(1)}) custom-call(s32[8]{0:T(128)S(1)} %get-tuple-element.20.len_ref, bf16[256,512]{1,0:T(8,128)(2,1)} %get-tuple-element.21.q_hbm, bf16[256,512]{1,0:T(8,128)(2,1)} %get-tuple-element.22.k_hbm, ...), custom_call_target="tpu_custom_call" | custom-call | flops 2147483648 | bytes 1572864 | tf_op jit(solution)/shard_map/cond/branch_0_fun/pallas_call | solution.py:375
  46.5 0.8 %copy.29 = f32[256,512]{1,0:T(8,128)} copy(f32[256,512]{1,0:T(8,128)S(1)} %get-tuple-element.58) | data formatting | bytes 1048576
  47.3 0.8 %copy.30 = f32[256,512]{1,0:T(8,128)} copy(f32[256,512]{1,0:T(8,128)S(1)} %get-tuple-element.59) | data formatting | bytes 1048576
  48.1 0.8 %copy.31 = f32[256,512]{1,0:T(8,128)} copy(f32[256,512]{1,0:T(8,128)S(1)} %get-tuple-element.60) | data formatting | bytes 1048576
  48.9 0.8 %copy.32 = f32[256,512]{1,0:T(8,128)} copy(f32[256,512]{1,0:T(8,128)S(1)} %get-tuple-element.61) | data formatting | bytes 1048576
Async XLA Ops:
  0.6 0.7 %copy-start = (s32[8]{0:T(128)S(1)}, s32[8]{0:T(128)}, u32[]{:S(2)}) copy-start(s32[8]{0:T(128)} %param.11) | copy-start | bytes 100
where the time goes:
time: 49.8 us; the launch traced here: 49.7 us
  Pallas kernels  43.8 us (88%)
  local copies, waits for them, and re-layouts  3.82 us (8%)
  between operations  1.3 us (3%)
  other arithmetic  0.73 us (1%)
    pallas_call x1, Pallas kernels, attention(): pl.pallas_call(functools.partial(kernel, n, first, far), out_shape=[out]...  43.8 us
    unnamed x6, local copies, waits for them, and re-layouts  3.82 us

commit v1 on v0

--- a/solution.py
+++ b/solution.py
@@ -113,43 +113,73 @@
             ld_own, ld_buf.at[d - 1], ld_ss.at[d - 1], ld_rs.at[d - 1], lax.rem(me + n - d, n)
         )
 
-    def pr_copy(src, w):
-        return remote(src, pr_buf.at[w], pr_ss.at[w], pr_rs.at[w], lax.rem(me + 2, n))
+    def pr_source(t):
+        return (t + 1 - first % 2) % 2 if t < first + 4 else t - 4
+
+    def pr_slot(t):
+        return 0 if t >= first + 4 else (t - first) // 2
+
+    def pr_copy(t, w):
+        source = pr_source(t)
+        if source == 0:
+            src = (k_hbm, v_hbm)[w].at[chunks[0]]
+        elif source == 1:
+            src = kv_buf.at[0, w, chunks[0]]
+        else:
+            src = pr_buf.at[w]
+        slot = pr_slot(t)
+        return remote(src, pr_buf.at[w], pr_ss.at[slot, w], pr_rs.at[w], t)
+
+    def pass_prompt(w):
+        for t in range(first, n):
+            @pl.when(me == pr_source(t))
+            def _(t=t):
+                pr_copy(t, w).start()
+
+    def take_prompt():
+        for w in (0, 1):
+            remote(pr_buf.at[w], pr_buf.at[w], pr_ss.at[0, w], pr_rs.at[w], first).wait_recv()
+            pass_prompt(w)
 
     def pg_copy():
         slot = lax.rem(me + n - first, n)
         return remote(pg_out, pg_buf.at[slot], pg_ss, pg_rs.at[slot], 0)
 
     distances = range(1, reach + 1)
-
     for c in range(len(chunks)):
         for d in distances:
             @pl.when(has_after(d))
             def _(d=d, c=c):
                 for w in (0, 1):
                     kv_copy(d, w, c).start()
+        if c == 0:
+            @pl.when(me == 0)
+            def _():
+                for w in (0, 1):
+                    pass_prompt(w)
+
+    direct, by_relay = parts[: len(parts) // 2], parts[len(parts) // 2 :]
 
     @pl.when(me == first - 1)
     def _():
-        for w, c in parts:
+        for w, c in by_relay:
             qd_to_relay(w, c).start()
-            for d in range(2, first):
+        for w, c in direct:
+            qd_copy(1, w, c).start()
+
+    for d in distances:
+        others = (me != first - 1) if d == 1 else (me >= 0)
+
+        @pl.when(has_before(d) & others)
+        def _(d=d):
+            for w, c in parts:
                 qd_copy(d, w, c).start()
 
-    for holder in (first - 2, first - 1):
-        @pl.when(me == holder)
-        def _(holder=holder):
-            for w in (0, 1):
-                kv_copy(holder, w, 0).wait_recv()
-                pr_copy(kv_buf.at[holder - 1, w, pl.ds(0, PROMPT)], w).start()
-
-    def pass_prompt():
+    @pl.when(me == 1)
+    def _():
         for w in (0, 1):
-            pr_copy(pr_buf.at[w], w).wait_recv()
-
-            @pl.when(me + 2 < n)
-            def _(w=w):
-                pr_copy(pr_buf.at[w], w).start()
+            kv_copy(1, w, 0).wait_recv()
+            pass_prompt(w)
 
     @pl.when(me == first)
     def _():
@@ -161,9 +191,9 @@
                 ).wait_recv()
                 qd_relayed(w, c).start()
 
-        relay(parts[: len(parts) // 2])
-        pass_prompt()
-        relay(parts[len(parts) // 2 :])
+        relay(by_relay[:2])
+        take_prompt()
+        relay(by_relay[2:])
 
     for copy in own_copies:
         copy.wait()
@@ -211,7 +241,7 @@
 
     @pl.when(me > first)
     def _():
-        pass_prompt()
+        take_prompt()
 
     @pl.when(me >= first)
     def _():
@@ -223,18 +253,12 @@
         @pl.when(has_before(d))
         def _(d=d):
             for w, c in parts:
-                if c == 0 and d in (first - 2, first - 1):
-                    @pl.when(me != d)
+                if c == 0 and d == 1:
+                    @pl.when(me != 1)
                     def _(w=w):
-                        kv_copy(d, w, 0).wait_recv()
+                        kv_copy(1, w, 0).wait_recv()
                 else:
                     kv_copy(d, w, c).wait_recv()
-            if d == 1:
-                for e in distances:
-                    @pl.when(has_before(e) & (me != first - 1))
-                    def _(e=e):
-                        for w, c in parts:
-                            qd_copy(e, w, c).start()
             mask = u_pos - d * rows >= t_start
 
             @pl.loop(0, heads, unroll=2)
@@ -345,13 +369,14 @@
 
     @pl.when(me == first)
     def _():
-        for w, c in parts:
+        for w, c in by_relay:
             qd_relayed(w, c).wait_send()
 
-    @pl.when((me >= first - 2) & (me + 2 < n))
-    def _():
-        for w in (0, 1):
-            pr_copy(pr_buf.at[w], w).wait_send()
+    for t in range(first, n):
+        @pl.when(me == pr_source(t))
+        def _(t=t):
+            for w in (0, 1):
+                pr_copy(t, w).wait_send()
 
     @pl.when(me >= first)
     def _():
@@ -396,7 +421,7 @@
             dma((reach, 2, cuts)), dma((reach, 2, cuts)),
             dma((reach, 2, cuts)), dma((reach, 2, cuts)),
             dma((reach,)), dma((reach,)),
-            dma((2,)), dma((2,)),
+            dma((2, 2)), dma((2,)),
             dma(()), dma((later,)),
             dma((2, cuts)), dma((2, cuts)), dma((4,)),
         ],
@@ -409,6 +434,36 @@
     )(doc_lengths, queries, keys, values, out_grad)
 
 
+def write_kernel(*refs):
+    count = len(refs) // 2
+    copies = []
+    for i in range(count):
+        half = refs[i].shape[0] // 2
+        for j in (0, 1):
+            part = pl.ds(j * half, half)
+            copies.append(
+                pltpu.make_async_copy(
+                    refs[i].at[part], refs[count + i].at[part], refs[-1].at[i, j]
+                )
+            )
+    for copy in copies:
+        copy.start()
+    for copy in copies:
+        copy.wait()
+
+
+def written(arrays):
+    hbm = pl.BlockSpec(memory_space=pltpu.HBM)
+    return pl.pallas_call(
+        write_kernel,
+        out_shape=[jax.ShapeDtypeStruct(a.shape, a.dtype) for a in arrays],
+        in_specs=[pl.BlockSpec(memory_space=pl.ANY)] * len(arrays),
+        out_specs=[hbm] * len(arrays),
+        scratch_shapes=[pltpu.SemaphoreType.DMA((len(arrays), 2))],
+        compiler_params=pltpu.CompilerParams(vmem_limit_bytes=2**20),
+    )(*arrays)
+
+
 def on_device(queries, keys, values, out_grad, doc_lengths):
     rows = queries.shape[0]
     docs = doc_lengths.shape[0]
@@ -416,12 +471,13 @@
     ends = jnp.sum(jnp.where(order[:, None] <= order[None, :], doc_lengths[:, None], 0), axis=0)
     span = (ends - 1) // rows - (ends - doc_lengths) // rows
     far = jnp.any((span > 1) & (order > 0))
-    return lax.cond(
+    arrays = lax.cond(
         far,
         functools.partial(attention, REACH),
         functools.partial(attention, 1),
         queries, keys, values, out_grad, doc_lengths,
     )
+    return tuple(written(arrays))
 
 
 def solution(mesh):

time: 49.8 us -> 45.3 us (0.910)
  local copies, waits for them, and re-layouts: 3.82 us -> 0.65 us
  Pallas kernels: 43.8 us -> 42.5 us
    unnamed x6 -> x2, local copies, waits for them, and re-layouts: 3.82 us -> 0.65 us
    pallas_call x1, Pallas kernels: 43.8 us -> 41.1 us  [attention(): pl.pallas_call(functools.partial(kernel, n, first, far), out_shape=[out]...]
    pallas_call x0 -> x1, Pallas kernels: none -> 1.38 us  [written(): pl.pallas_call(write_kernel, out_shape=[jax.ShapeDtypeStruct(a.shape, a.d...]
where the time goes in v1:
time: 45.3 us; the launch traced here: 45.2 us
  Pallas kernels  42.5 us (94%)
  between operations  1.3 us (3%)
  other arithmetic  0.73 us (2%)
  local copies, waits for them, and re-layouts  0.65 us (1%)
    pallas_call x1, Pallas kernels, attention(): pl.pallas_call(functools.partial(kernel, n, first, far), out_shape=[out]...  41.1 us
    pallas_call x1, Pallas kernels, written(): pl.pallas_call(write_kernel, out_shape=[jax.ShapeDtypeStruct(a.shape, a.d...  1.38 us

profile of v1, /device:TPU:0, one launch (start us, length us, event | category | flops | bytes accessed | tf_op | source)
XLA Modules:
  0.0 45.2 jit_solution(10433534223974073394)
XLA Ops:
  0.6 0.0 copy-start
  0.6 0.6 %copy-done = s32[8]{0:T(128)S(1)} copy-done((s32[8]{0:T(128)S(1)}, s32[8]{0:T(128)}, u32[]{:S(2)}) %copy-start) | copy-done | bytes 56
  1.3 0.1 select_reduce_fusion
  1.4 0.6 %and_reduce_fusion = pred[]{:T(512)} fusion(s32[8]{0:T(128)S(1)} %select_reduce_fusion, s32[8]{0:T(128)S(1)} %copy-done), kind=kLoop, calls=%fused_computation.2 | loop fusion | flops 295 | bytes 65 | tf_op jit(solution)/shard_map/reduce_or | solution.py:473
  2.7 41.1 %conditional.1 = ((f32[256,512]{1,0:T(8,128)S(1)}, f32[256,512]{1,0:T(8,128)S(1)}, f32[256,512]{1,0:T(8,128)S(1)}, f32[256,512]{1,0:T(8,128)S(1)})) conditional(s32[]{:T(128)} %convert_element_type.3, (s32[8]{0:T(128)S(1)}, bf16[256,512]{1,0:T(8,128)(2,1)}, bf16[256,512]{1,0:T(8,128)(2,1)}, bf16[256,512]{1,0:T(8,128)(2,1)}, ...), branch_computations={%region_2.3_spmd, %region_3.4_spmd} | conditional | flops 2147483648 | bytes 1572872 | solution.py:474
  2.7 41.1 %branch_0_fun.1 = (f32[256,512]{1,0:T(8,128)S(1)}, f32[256,512]{1,0:T(8,128)S(1)}, f32[256,512]{1,0:T(8,128)S(1)}, f32[256,512]{1,0:T(8,128)S(1)}) custom-call(s32[8]{0:T(128)S(1)} %get-tuple-element.20.len_ref, bf16[256,512]{1,0:T(8,128)(2,1)} %get-tuple-element.21.q_hbm, bf16[256,512]{1,0:T(8,128)(2,1)} %get-tuple-element.22.k_hbm, ...), custom_call_target="tpu_custom_call" | custom-call | flops 2147483648 | bytes 1572864 | tf_op jit(solution)/shard_map/cond/branch_0_fun/pallas_call | solution.py:400
  43.8 1.4 %shard_map.84 = (f32[256,512]{1,0:T(8,128)}, f32[256,512]{1,0:T(8,128)}, f32[256,512]{1,0:T(8,128)}, f32[256,512]{1,0:T(8,128)}) custom-call(f32[256,512]{1,0:T(8,128)S(1)} %get-tuple-element.38.refs_0_, f32[256,512]{1,0:T(8,128)S(1)} %get-tuple-element.39.refs_1_, f32[256,512]{1,0:T(8,128)S(1)} %get-tuple-element.40.refs_2_, ...), custom_call_target="tpu_custom_call" | custom-call | tf_op jit(solution)/shard_map/pallas_call | solution.py:457
Async XLA Ops:
  0.6 0.7 %copy-start = (s32[8]{0:T(128)S(1)}, s32[8]{0:T(128)}, u32[]{:S(2)}) copy-start(s32[8]{0:T(128)} %param.11) | copy-start | bytes 100

commit v2 on v1

--- a/solution.py
+++ b/solution.py
@@ -167,13 +167,16 @@
         for w, c in direct:
             qd_copy(1, w, c).start()
 
-    for d in distances:
-        others = (me != first - 1) if d == 1 else (me >= 0)
-
-        @pl.when(has_before(d) & others)
-        def _(d=d):
-            for w, c in parts:
-                qd_copy(d, w, c).start()
+    def send_qd(d):
+        for w, c in parts:
+            qd_copy(d, w, c).start()
+
+    for d in range(2, first):
+        pl.when(me == first - 1)(functools.partial(send_qd, d))
+    for d in range(1, first - 1):
+        @pl.when((me >= d) & (me < first - 1))
+        def _(d=d):
+            send_qd(d)
 
     @pl.when(me == 1)
     def _():
@@ -211,7 +214,11 @@
     t_start = doc_start(t_pos)
 
     def hs(h):
-        return pl.ds(pl.multiple_of(h * HD, HD), HD)
+        return pl.ds(h * HD, HD)
+
+    def each_head(body):
+        for h in range(heads):
+            body(h)
 
     def forward(h, keys, values, mask):
         s = dot_nt(keys, q_ref[:, hs(h)]) * SCALE2
@@ -228,7 +235,7 @@
 
     own_mask = (u_pos <= t_pos) & (u_pos >= t_start)
 
-    @pl.loop(0, heads, unroll=2)
+    @each_head
     def _(h):
         s = dot_nt(k_ref[:, hs(h)], q_ref[:, hs(h)]) * SCALE2
         s = jnp.where(own_mask, s, NEG_FILL)
@@ -245,9 +252,14 @@
 
     @pl.when(me >= first)
     def _():
-        @pl.loop(0, heads, unroll=2)
+        @each_head
         def _(h):
             sp_buf[h] = forward(h, pr_buf[0, :, hs(h)], pr_buf[1, :, hs(h)], None)
+
+    for d in range(1, far + 1):
+        @pl.when(me >= first + d)
+        def _(d=d):
+            send_qd(d)
 
     for d in distances:
         @pl.when(has_before(d))
@@ -261,13 +273,13 @@
                     kv_copy(d, w, c).wait_recv()
             mask = u_pos - d * rows >= t_start
 
-            @pl.loop(0, heads, unroll=2)
+            @each_head
             def _(h):
                 s_buf[d, h] = forward(
                     h, kv_buf[d - 1, 0, :, hs(h)], kv_buf[d - 1, 1, :, hs(h)], mask
                 )
 
-    @pl.loop(0, heads, unroll=2)
+    @each_head
     def _(h):
         total = tot_ref[pl.ds(h, 1)]
         out = out_t[h] / total
@@ -293,7 +305,7 @@
 
     @pl.when(me >= first)
     def _():
-        @pl.loop(0, heads, unroll=2)
+        @each_head
         def _(h):
             p, ds = own_backward(h, sp_buf[h], pr_buf[1, :, hs(h)])
             pg_out[0, :, hs(h)] = dot_nn(ds, q_ref[:, hs(h)]).astype(jnp.bfloat16)
@@ -306,7 +318,7 @@
     def _():
         dq_t[...] = jnp.zeros_like(dq_t)
 
-    @pl.loop(0, heads, unroll=2)
+    @each_head
     def _(h):
         p, ds = own_backward(h, s_buf[0, h], v_ref[:, hs(h)])
         dk_ref[:, hs(h)] = dot_nn(ds, q_ref[:, hs(h)])
@@ -316,12 +328,12 @@
     for d in distances:
         @pl.when(has_before(d))
         def _(d=d):
-            @pl.loop(0, heads, unroll=2)
+            @each_head
             def _(h):
                 p, ds = own_backward(h, s_buf[d, h], kv_buf[d - 1, 1, :, hs(h)])
                 dq_t[h] += dot_tn(kv_buf[d - 1, 0, :, hs(h)], ds)
 
-    @pl.loop(0, heads, unroll=2)
+    @each_head
     def _(h):
         dq_ref[:, hs(h)] = jnp.transpose(dq_t[h] * SCALE)
 
@@ -333,7 +345,7 @@
             ld_copy(d).wait_recv()
             mask = u_pos >= doc_start(t_pos + d * rows)
 
-            @pl.loop(0, heads, unroll=2)
+            @each_head
             def _(h):
                 q = qd_buf[d - 1, 0, :, hs(h)]
                 g = qd_buf[d - 1, 1, :, hs(h)]

time: 45.3 us -> 44.3 us (0.978)
  the two profiles are of different devices: /device:TPU:0 before, /device:TPU:24 now
where the time goes in v2:
time: 44.3 us; the launch traced here: 44.1 us
  Pallas kernels  41 us (93%)
  between operations  1.48 us (3%)
  other arithmetic  0.73 us (2%)
  local copies, waits for them, and re-layouts  0.65 us (1%)
    pallas_call x1, Pallas kernels, attention(): pl.pallas_call(functools.partial(kernel, n, first, far), out_shape=[out]...  39.6 us
    pallas_call x1, Pallas kernels, written(): pl.pallas_call(write_kernel, out_shape=[jax.ShapeDtypeStruct(a.shape, a.d...  1.38 us

profile of v2, /device:TPU:24, one launch (start us, length us, event | category | flops | bytes accessed | tf_op | source)
XLA Modules:
  0.0 44.1 jit_solution(2345244482483723692)
XLA Ops:
  0.6 0.0 copy-start
  0.6 0.6 %copy-done = s32[8]{0:T(128)S(1)} copy-done((s32[8]{0:T(128)S(1)}, s32[8]{0:T(128)}, u32[]{:S(2)}) %copy-start) | copy-done | bytes 56
  1.3 0.1 select_reduce_fusion
  1.4 0.6 %and_reduce_fusion = pred[]{:T(512)} fusion(s32[8]{0:T(128)S(1)} %select_reduce_fusion, s32[8]{0:T(128)S(1)} %copy-done), kind=kLoop, calls=%fused_computation.2 | loop fusion | flops 295 | bytes 65 | tf_op jit(solution)/shard_map/reduce_or | solution.py:485
  2.7 39.9 %conditional.1 = ((f32[256,512]{1,0:T(8,128)S(1)}, f32[256,512]{1,0:T(8,128)S(1)}, f32[256,512]{1,0:T(8,128)S(1)}, f32[256,512]{1,0:T(8,128)S(1)})) conditional(s32[]{:T(128)} %convert_element_type.3, (s32[8]{0:T(128)S(1)}, bf16[256,512]{1,0:T(8,128)(2,1)}, bf16[256,512]{1,0:T(8,128)(2,1)}, bf16[256,512]{1,0:T(8,128)(2,1)}, ...), branch_computations={%region_2.3_spmd, %region_3.4_spmd} | conditional | flops 2147483648 | bytes 1572872 | solution.py:486
  2.7 39.6 %branch_0_fun.1 = (f32[256,512]{1,0:T(8,128)S(1)}, f32[256,512]{1,0:T(8,128)S(1)}, f32[256,512]{1,0:T(8,128)S(1)}, f32[256,512]{1,0:T(8,128)S(1)}) custom-call(s32[8]{0:T(128)S(1)} %get-tuple-element.20.len_ref, bf16[256,512]{1,0:T(8,128)(2,1)} %get-tuple-element.21.q_hbm, bf16[256,512]{1,0:T(8,128)(2,1)} %get-tuple-element.22.k_hbm, ...), custom_call_target="tpu_custom_call" | custom-call | flops 2147483648 | bytes 1572864 | tf_op jit(solution)/shard_map/cond/branch_0_fun/pallas_call | solution.py:412
  42.5 1.4 %shard_map.84 = (f32[256,512]{1,0:T(8,128)}, f32[256,512]{1,0:T(8,128)}, f32[256,512]{1,0:T(8,128)}, f32[256,512]{1,0:T(8,128)}) custom-call(f32[256,512]{1,0:T(8,128)S(1)} %get-tuple-element.38.refs_0_, f32[256,512]{1,0:T(8,128)S(1)} %get-tuple-element.39.refs_1_, f32[256,512]{1,0:T(8,128)S(1)} %get-tuple-element.40.refs_2_, ...), custom_call_target="tpu_custom_call" | custom-call | tf_op jit(solution)/shard_map/pallas_call | solution.py:469
Async XLA Ops:
  0.6 0.7 %copy-start = (s32[8]{0:T(128)S(1)}, s32[8]{0:T(128)}, u32[]{:S(2)}) copy-start(s32[8]{0:T(128)} %param.11) | copy-start | bytes 100
